TPU v7x, 32 devices: a whole 2x2x4 slice. The times are simulated.
32 devices in a mesh: groups: 2 (over x), query: 16 (over z, y, core).
Axes of the slice: x: 2, y: 2, z: 4, core: 2. Of those that a mesh axis runs over, the one named last changes fastest.
Arguments:
- tokens: bfloat16 [384, 4096], P(('groups', 'query')), parts along dimension 0, may hold values from -6 to 6
- grad_out: bfloat16 [384, 4096], P(('groups', 'query')), parts along dimension 0, may hold values from -6 to 6
- gate_weight: bfloat16 [4096, 14336], P(None, 'query'), may hold values from -0.09375 to 0.09375
- up_weight: bfloat16 [4096, 14336], P(None, 'query'), may hold values from -0.09375 to 0.09375
- query_left: bfloat16 [16, 4096, 32], P('query'), may hold values from -0.09375 to 0.09375
- query_right: bfloat16 [16, 14336, 32], P('query'), may hold values from -0.09375 to 0.09375
Outputs:
- scores: float32 [384, 16], P(('groups', 'query')), parts along dimension 0
There are 2 independent parts, one for each index of `groups`. A program takes and returns all parts, laid end to end along the dimension named above; an argument that names none is the same for every part. Nothing has to cross between parts.
All inputs are finite; a program needn't handle non-finite values.
Results may differ from a plain program's by a relative error of at most 0.0003.
Values may be sent and summed in bfloat16 or wider, within the bound.
No kernel may reach another device: no remote copies, remote signals or barrier semaphores. Data moves between devices by JAX's collectives and lax.ppermute only.
A program may use at most 128 MiB of HBM per device.

v0:
```python
import jax
import jax.numpy as jnp
from jax import lax
from jax.sharding import PartitionSpec as P


def body(tokens, grad_out, gate_weight, up_weight, query_left, query_right):
    whole = lax.all_gather(tokens, "query", axis=0, tiled=True)
    right_cols = lax.all_to_all(query_right, "query", split_axis=1, concat_axis=0, tiled=True)
    right_wide = right_cols.astype(jnp.float32)
    num_queries = right_cols.shape[0]
    rank_size = right_cols.shape[2]
    tok_rows = tokens.shape[0]
    gate = jnp.dot(whole, gate_weight, preferred_element_type=jnp.float32)
    up = jnp.dot(whole, up_weight, preferred_element_type=jnp.float32)
    hidden = jax.nn.silu(gate) * up
    term = jnp.einsum("tf,qfr->tqr", hidden, right_wide, precision=lax.Precision.HIGHEST)
    proj_right = lax.psum_scatter(
        term.reshape(tok_rows * lax.axis_size("query"), num_queries * rank_size),
        "query",
        scatter_dimension=0,
        tiled=True,
    )
    proj_right = proj_right.reshape(tok_rows, num_queries, rank_size)
    left = jnp.einsum(
        "td,kdr->tkr",
        grad_out,
        lax.all_gather(query_left, "query", axis=0, tiled=True),
        preferred_element_type=jnp.float32,
    )
    return jnp.sum(left * proj_right, axis=2)


def solution(mesh):
    return jax.shard_map(
        body,
        mesh=mesh,
        in_specs=(
            P(("groups", "query"), None),
            P(("groups", "query"), None),
            P(None, "query"),
            P(None, "query"),
            P("query", None, None),
            P("query", None, None),
        ),
        out_specs=P(("groups", "query"), None),
        check_vma=False,
    )
```

profile of v0, /device:TPU:17, one launch (start us, length us, event | category | flops | bytes accessed | tf_op | source)
XLA Modules:
  0.0 230.3 jit_solution(11249629762622206637)
XLA Ops:
  6.5 0.7 all-gather.6.cloned.1.call-update
  7.3 0.0 all-gather.4.cloned.1.call-start
  7.3 0.7 all-gather.4.cloned.1.call-update
  8.0 14.3 %copy.10 = bf16[1,14336,32]{2,0,1:T(2,128)(2,1)} copy(bf16[1,14336,32]{1,2,0:T(8,128)(2,1)} %param.11) | data formatting | bytes 1835008 | tf_op args[5]
  22.3 0.5 broadcast.2
  22.8 79.8 %reduce = bf16[14336,32]{1,0:T(8,128)(2,1)} reduce(bf16[14336,1,32]{2,1,0:T(2,128)(2,1)} %bitcast.26, bf16[]{:T(256)} %broadcast.2), dimensions={1}, to_apply=%bitcast.15.reduce_sub_computation | reduce | bytes 1835010
  102.6 5.0 %reshape.13 = bf16[16,2,14336]{2,1,0:T(2,128)(2,1)S(1)} reshape(bf16[14336,32]{1,0:T(8,128)(2,1)} %reduce) | data formatting | bytes 1835008
  107.5 27.9 %all_to_all.12 = bf16[16,2,14336]{2,1,0:T(2,128)(2,1)S(1)} all-to-all(bf16[16,2,14336]{2,1,0:T(2,128)(2,1)S(1)} %reshape.13), channel_id=1, replica_groups=mesh['groups'=2,'query'=16] {'query'}, dimensions={0} | all-to-all | bytes 1835008 | tf_op jit(solution)/shard_map/all_to_all | solution.py:9
  135.4 8.4 %reshape.14 = bf16[14336,1,32]{2,1,0:T(2,128)(2,1)} reshape(bf16[16,2,14336]{2,1,0:T(2,128)(2,1)S(1)} %all_to_all.12) | data formatting | bytes 1835008
  143.8 13.7 %copy.11 = bf16[1,14336,32]{1,2,0:T(8,128)(2,1)S(1)} copy(bf16[1,14336,32]{2,0,1:T(2,128)(2,1)} %bitcast.27) | data formatting | bytes 1835008 | tf_op jit(solution)/shard_map/all_to_all | solution.py:9
  157.5 0.1 copy.15
  157.6 0.2 copy.12
  157.8 0.0 all-gather.6.cloned.1.call-done
  157.8 2.5 %reshape.10 = bf16[192,4096]{1,0:T(8,128)(2,1)S(1)} reshape(bf16[16,12,4096]{2,1,0:T(8,128)(2,1)} %all-gather.6.cloned.1.call-done) | data formatting | bytes 3145728
  160.3 4.9 %fusion.4 = f32[192,896]{1,0:T(8,128)S(1)} fusion(bf16[192,4096]{1,0:T(8,128)(2,1)S(1)} %reshape.10, bf16[4096,896]{1,0:T(8,128)(2,1)} %param.8), kind=kOutput, calls=%fused_computation.6 | convolution fusion | flops 1409286144 | bytes 9601024 | tf_op jit(solution)/shard_map/dot_general | solution.py:14
  165.2 0.0 copy-start.1
  165.2 4.9 %convolution_multiply_fusion = f32[192,896]{1,0:T(8,128)S(1)} fusion(bf16[192,4096]{1,0:T(8,128)(2,1)S(1)} %reshape.10, bf16[4096,896]{1,0:T(8,128)(2,1)} %param.9, f32[192,896]{1,0:T(8,128)S(1)} %fusion.4), kind=kOutput, calls=%fused_computation | convolution fusion | flops 1410146304 | bytes 10289152 | tf_op jit(solution)/shard_map/dot_general | solution.py:15
  170.1 1.1 fusion.5
  171.2 25.9 %fusion = f32[16,512]{1,0:T(8,128)S(1)} fusion(f32[192,512]{1,0:T(8,128)S(1)} %fusion.5), kind=kCustom, calls=%all-reduce-scatter | all-reduce-scatter fusion | flops 131073 | bytes 426496
  197.1 2.8 %collective-permute-start = (f32[16,512]{1,0:T(8,128)S(1)}, f32[16,512]{1,0:T(8,128)S(1)}, u32[]{:S(2)}, u32[]{:S(2)}) collective-permute-start(f32[16,512]{1,0:T(8,128)S(1)} %fusion), channel_id=1, source_target_pairs={{0,1},{1,2},{2,3},{3,4},{4,5},{5,6},{6,7},{7,8},{8,9},{9,10},{10,1... | collective-permute-start | bytes 98312
  199.9 5.0 %collective-permute-start.1 = (f32[16,512]{1,0:T(8,128)S(1)}, f32[16,512]{1,0:T(8,128)S(1)}, u32[]{:S(2)}, u32[]{:S(2)}) collective-permute-start(f32[16,512]{1,0:T(8,128)S(1)} %fusion), channel_id=1, source_target_pairs={{0,2},{1,3},{2,4},{3,5},{4,6},{5,7},{6,8},{7,9},{8,10},{9,11},{10,... | collective-permute-start | bytes 98312
  204.8 7.5 %collective-permute-start.2 = (f32[16,512]{1,0:T(8,128)S(1)}, f32[16,512]{1,0:T(8,128)S(1)}, u32[]{:S(2)}, u32[]{:S(2)}) collective-permute-start(f32[16,512]{1,0:T(8,128)S(1)} %fusion), channel_id=1, source_target_pairs={{0,3},{1,4},{2,5},{3,6},{4,7},{5,8},{6,9},{7,10},{8,11},{9,12},{10... | collective-permute-start | bytes 98312
  212.3 1.9 collective-permute-start.3
  214.3 0.6 dynamic-slice.4
  215.5 1.5 collective-permute-done.3
  217.0 0.0 collective-permute-done
  217.0 0.0 collective-permute-done.1
  217.0 0.5 concatenate
  217.5 0.1 reshape.8
  217.6 0.0 all-gather.4.cloned.1.call-done
  217.6 5.1 %fusion.3 = f32[12,16]{0,1:T(8,128)S(1)} fusion(f32[12,16,32]{2,1,0:T(8,128)S(1)} %reshape.8, bf16[16,4096,32]{1,2,0:T(8,128)(2,1)} %all-gather.4.cloned.1.call-done, bf16[12,4096]{1,0:T(8,128)(2,1)S(1)} %copy-done), kind=kOutput, calls=%fused_computation.4 | convolution fusion | flops 50343744 | bytes 4317952 | tf_op jit(solution)/shard_map/td,kdr->tkr/dot_general | solution.py:25
  222.7 0.7 copy.14
  (7 shorter events, 0.0 us)
Async XLA Ops:
  6.5 211.1 %copy-start = (bf16[12,4096]{1,0:T(8,128)(2,1)S(1)}, bf16[12,4096]{1,0:T(8,128)(2,1)}, u32[]{:S(2)}) copy-start(bf16[12,4096]{1,0:T(8,128)(2,1)} %param.7) | copy-start | bytes 294916
  6.5 151.2 %all-gather.6.cloned.1.call-start = ((), (), s32[]{:S(2)}) async-start(), calls=%async_computation.2 | async-start | bytes 2228224 | tf_op jit(solution)/shard_map/all_gather | solution.py:8
  7.3 210.4 %all-gather.4.cloned.1.call-start = ((), (), s32[]{:S(2)}) async-start(), calls=%async_computation.1 | async-start | bytes 4456448 | tf_op jit(solution)/shard_map/all_gather | solution.py:28
  165.2 49.1 %copy-start.1 = (u32[32]{0:T(128)S(1)}, u32[32]{0:T(128)}, u32[]{:S(2)}) copy-start(u32[32]{0:T(128)} %constant.11) | copy-start | bytes 388
  197.1 19.9 %collective-permute-start = (f32[16,512]{1,0:T(8,128)S(1)}, f32[16,512]{1,0:T(8,128)S(1)}, u32[]{:S(2)}, u32[]{:S(2)}) collective-permute-start(f32[16,512]{1,0:T(8,128)S(1)} %fusion), channel_id=1, source_target_pairs={{0,1},{1,2},{2,3},{3,4},{4,5},{5,6},{6,7},{7,8},{8,9},{9,10},{10,1... | collective-permute-start | bytes 98312
  199.9 17.1 %collective-permute-start.1 = (f32[16,512]{1,0:T(8,128)S(1)}, f32[16,512]{1,0:T(8,128)S(1)}, u32[]{:S(2)}, u32[]{:S(2)}) collective-permute-start(f32[16,512]{1,0:T(8,128)S(1)} %fusion), channel_id=1, source_target_pairs={{0,2},{1,3},{2,4},{3,5},{4,6},{5,7},{6,8},{7,9},{8,10},{9,11},{10,... | collective-permute-start | bytes 98312
  204.8 12.1 %collective-permute-start.2 = (f32[16,512]{1,0:T(8,128)S(1)}, f32[16,512]{1,0:T(8,128)S(1)}, u32[]{:S(2)}, u32[]{:S(2)}) collective-permute-start(f32[16,512]{1,0:T(8,128)S(1)} %fusion), channel_id=1, source_target_pairs={{0,3},{1,4},{2,5},{3,6},{4,7},{5,8},{6,9},{7,10},{8,11},{9,12},{10... | collective-permute-start | bytes 98312
  212.3 4.7 %collective-permute-start.3 = (f32[12,512]{1,0:T(8,128)S(1)}, f32[12,512]{1,0:T(8,128)S(1)}, u32[]{:S(2)}, u32[]{:S(2)}) collective-permute-start(f32[12,512]{1,0:T(8,128)S(1)} %slice), channel_id=1, source_target_pairs={{0,4},{1,5},{2,6},{3,7},{4,8},{5,9},{6,10},{7,11},{8,12},{9,13},{1... | collective-permute-start | bytes 73736
Sparse Core Ops, SparseCore 0:
  9.5 41.0 all-gather.5
  52.8 50.6 all-gather.3
where the time goes:
time: 232 us; the launch traced here: 230 us
  other arithmetic  79.8 us (34%)
  blocking collectives  53.8 us (23%)
  local copies, waits for them, and re-layouts  46.4 us (20%)
  starting transfers between devices  17.2 us (7%)
  matrix products  16 us (7%)
  between operations  14.2 us (6%)
  waiting for transfers between devices  2.94 us (1%)
    unnamed x1, other arithmetic  79.8 us
    unnamed x14, local copies, waits for them, and re-layouts  31.8 us
    all_to_all x1, blocking collectives, body(): lax.all_to_all(query_right, 'query', split_axis=1, concat_axis=0, tiled=T...  27.9 us
    unnamed x1, blocking collectives  25.9 us
    unnamed x4, starting transfers between devices  17.1 us
    all_to_all x1, local copies, waits for them, and re-layouts, body(): lax.all_to_all(query_right, 'query', split_axis=1, concat_axis=0, tiled=T...  13.7 us
    dot_general x1, matrix products, body(): jnp.einsum('td,kdr->tkr', grad_out, lax.all_gather(query_left, 'query', a...  5.07 us
    dot_general x1, matrix products, body(): up = jnp.dot(whole, up_weight, preferred_element_type=jnp.float32)  4.93 us
  transfers between devices with their start and end apart: 6, of which 1 were waited for; matrix products, arithmetic and copies ran while one was open for 70% of the time, Pallas kernels for 0%

commit v1 on v0

--- a/solution.py
+++ b/solution.py
@@ -6,7 +6,12 @@
 
 def body(tokens, grad_out, gate_weight, up_weight, query_left, query_right):
     whole = lax.all_gather(tokens, "query", axis=0, tiled=True)
-    right_cols = lax.all_to_all(query_right, "query", split_axis=1, concat_axis=0, tiled=True)
+    right_cols = jnp.concatenate(
+        lax.all_to_all(
+            jnp.stack(jnp.split(query_right, lax.axis_size("query"), axis=1)), "query", 0, 0
+        ),
+        axis=0,
+    )
     right_wide = right_cols.astype(jnp.float32)
     num_queries = right_cols.shape[0]
     rank_size = right_cols.shape[2]

time: 232 us -> 137 us (0.59)
  other arithmetic: 79.8 us -> 0 us
  blocking collectives: 53.8 us -> 31 us
  waiting for transfers between devices: 2.94 us -> 25.2 us
  local copies, waits for them, and re-layouts: 46.4 us -> 27.4 us
  starting transfers between devices: 17.2 us -> 21.6 us
    unnamed x1 -> x0, other arithmetic: 79.8 us -> none
    all_to_all x1 -> x0, blocking collectives: 27.9 us -> none  [body(): lax.all_to_all(query_right, 'query', split_axis=1, concat_axis=0, tiled=T...]
    all_gather x1, waiting for transfers between devices: 0.02 us -> 22.3 us  [body(): whole = lax.all_gather(tokens, 'query', axis=0, tiled=True)]
    all_to_all x1 -> x0, local copies, waits for them, and re-layouts: 13.7 us -> none  [body(): lax.all_to_all(query_right, 'query', split_axis=1, concat_axis=0, tiled=T...]
    unnamed x14 -> x24, local copies, waits for them, and re-layouts: 31.8 us -> 25.2 us
    all_to_all x0 -> x1, starting transfers between devices: none -> 6.5 us  [body(): lax.all_to_all(jnp.stack(jnp.split(query_right, lax.axis_size('query'), a...]
    unnamed x1, blocking collectives: 25.9 us -> 31 us
  transfers between devices with their start and end apart: 6 -> 7, of which waited for: 1 -> 2; matrix products, arithmetic and copies ran while one was open for 70% -> 51% of each run, Pallas kernels for 0% -> 0%
where the time goes in v1:
time: 137 us; the launch traced here: 136 us
  blocking collectives  31 us (23%)
  local copies, waits for them, and re-layouts  27.4 us (20%)
  waiting for transfers between devices  25.2 us (18%)
  starting transfers between devices  21.6 us (16%)
  matrix products  16.1 us (12%)
  between operations  14.2 us (10%)
    unnamed x1, blocking collectives  31 us
    unnamed x24, local copies, waits for them, and re-layouts  25.2 us
    all_gather x1, waiting for transfers between devices, body(): whole = lax.all_gather(tokens, 'query', axis=0, tiled=True)  22.3 us
    unnamed x4, starting transfers between devices  15.1 us
    all_to_all x1, starting transfers between devices, body(): lax.all_to_all(jnp.stack(jnp.split(query_right, lax.axis_size('query'), a...  6.5 us
    dot_general x1, matrix products, body(): jnp.einsum('td,kdr->tkr', grad_out, lax.all_gather(query_left, 'query', a...  5.07 us
    dot_general x1, matrix products, body(): up = jnp.dot(whole, up_weight, preferred_element_type=jnp.float32)  4.97 us
    dot_general x1, matrix products, body(): gate = jnp.dot(whole, gate_weight, preferred_element_type=jnp.float32)  4.93 us
  transfers between devices with their start and end apart: 7, of which 2 were waited for; matrix products, arithmetic and copies ran while one was open for 51% of the time, Pallas kernels for 0%

profile of v1, /device:TPU:17, one launch (start us, length us, event | category | flops | bytes accessed | tf_op | source)
XLA Modules:
  0.0 135.6 jit_solution(7202075361333530947)
XLA Ops:
  6.5 0.7 all-gather.6.cloned.1.call-update
  7.3 0.7 all-gather.4.cloned.1.call-update
  8.0 1.4 %bitcast_dynamic-update-slice_fusion.15 = bf16[16,1,896,32]{2,3,1,0:T(8,128)(2,1)} fusion(bf16[1,14336,32]{1,2,0:T(8,128)(2,1)} %param.11), kind=kLoop, calls=%fused_computation.20 | loop fusion | bytes 114688
  9.5 1.4 %bitcast_dynamic-update-slice_fusion.14 = bf16[16,1,896,32]{2,3,1,0:T(8,128)(2,1)} fusion(bf16[16,1,896,32]{2,3,1,0:T(8,128)(2,1)} %bitcast_dynamic-update-slice_fusion.15, bf16[1,14336,32]{1,2,0:T(8,128)(2,1)} %param.11), kind=kLoop, calls=%fused_computation.19 | loop fusion | bytes 114688
  10.9 1.4 %bitcast_dynamic-update-slice_fusion.13 = bf16[16,1,896,32]{2,3,1,0:T(8,128)(2,1)} fusion(bf16[16,1,896,32]{2,3,1,0:T(8,128)(2,1)} %bitcast_dynamic-update-slice_fusion.14, bf16[1,14336,32]{1,2,0:T(8,128)(2,1)} %param.11), kind=kLoop, calls=%fused_computation.18 | loop fusion | bytes 114688
  12.3 1.4 %bitcast_dynamic-update-slice_fusion.12 = bf16[16,1,896,32]{2,3,1,0:T(8,128)(2,1)} fusion(bf16[16,1,896,32]{2,3,1,0:T(8,128)(2,1)} %bitcast_dynamic-update-slice_fusion.13, bf16[1,14336,32]{1,2,0:T(8,128)(2,1)} %param.11), kind=kLoop, calls=%fused_computation.17 | loop fusion | bytes 114688
  13.8 1.4 %bitcast_dynamic-update-slice_fusion.11 = bf16[16,1,896,32]{2,3,1,0:T(8,128)(2,1)} fusion(bf16[16,1,896,32]{2,3,1,0:T(8,128)(2,1)} %bitcast_dynamic-update-slice_fusion.12, bf16[1,14336,32]{1,2,0:T(8,128)(2,1)} %param.11), kind=kLoop, calls=%fused_computation.16 | loop fusion | bytes 114688
  15.2 1.4 %bitcast_dynamic-update-slice_fusion.10 = bf16[16,1,896,32]{2,3,1,0:T(8,128)(2,1)} fusion(bf16[16,1,896,32]{2,3,1,0:T(8,128)(2,1)} %bitcast_dynamic-update-slice_fusion.11, bf16[1,14336,32]{1,2,0:T(8,128)(2,1)} %param.11), kind=kLoop, calls=%fused_computation.15 | loop fusion | bytes 114688
  16.7 1.4 %bitcast_dynamic-update-slice_fusion.9 = bf16[16,1,896,32]{2,3,1,0:T(8,128)(2,1)} fusion(bf16[16,1,896,32]{2,3,1,0:T(8,128)(2,1)} %bitcast_dynamic-update-slice_fusion.10, bf16[1,14336,32]{1,2,0:T(8,128)(2,1)} %param.11), kind=kLoop, calls=%fused_computation.14 | loop fusion | bytes 114688
  18.1 1.4 %bitcast_dynamic-update-slice_fusion.8 = bf16[16,1,896,32]{2,3,1,0:T(8,128)(2,1)} fusion(bf16[16,1,896,32]{2,3,1,0:T(8,128)(2,1)} %bitcast_dynamic-update-slice_fusion.9, bf16[1,14336,32]{1,2,0:T(8,128)(2,1)} %param.11), kind=kLoop, calls=%fused_computation.13 | loop fusion | bytes 114688
  19.5 1.4 %bitcast_dynamic-update-slice_fusion.7 = bf16[16,1,896,32]{2,3,1,0:T(8,128)(2,1)} fusion(bf16[16,1,896,32]{2,3,1,0:T(8,128)(2,1)} %bitcast_dynamic-update-slice_fusion.8, bf16[1,14336,32]{1,2,0:T(8,128)(2,1)} %param.11), kind=kLoop, calls=%fused_computation.12 | loop fusion | bytes 114688
  21.0 1.4 %bitcast_dynamic-update-slice_fusion.6 = bf16[16,1,896,32]{2,3,1,0:T(8,128)(2,1)} fusion(bf16[16,1,896,32]{2,3,1,0:T(8,128)(2,1)} %bitcast_dynamic-update-slice_fusion.7, bf16[1,14336,32]{1,2,0:T(8,128)(2,1)} %param.11), kind=kLoop, calls=%fused_computation.11 | loop fusion | bytes 114688
  22.4 1.4 %bitcast_dynamic-update-slice_fusion.5 = bf16[16,1,896,32]{2,3,1,0:T(8,128)(2,1)} fusion(bf16[16,1,896,32]{2,3,1,0:T(8,128)(2,1)} %bitcast_dynamic-update-slice_fusion.6, bf16[1,14336,32]{1,2,0:T(8,128)(2,1)} %param.11), kind=kLoop, calls=%fused_computation.10 | loop fusion | bytes 114688
  23.9 1.4 %bitcast_dynamic-update-slice_fusion.4 = bf16[16,1,896,32]{2,3,1,0:T(8,128)(2,1)} fusion(bf16[16,1,896,32]{2,3,1,0:T(8,128)(2,1)} %bitcast_dynamic-update-slice_fusion.5, bf16[1,14336,32]{1,2,0:T(8,128)(2,1)} %param.11), kind=kLoop, calls=%fused_computation.9 | loop fusion | bytes 114688
  25.3 1.4 %bitcast_dynamic-update-slice_fusion.3 = bf16[16,1,896,32]{2,3,1,0:T(8,128)(2,1)} fusion(bf16[16,1,896,32]{2,3,1,0:T(8,128)(2,1)} %bitcast_dynamic-update-slice_fusion.4, bf16[1,14336,32]{1,2,0:T(8,128)(2,1)} %param.11), kind=kLoop, calls=%fused_computation.8 | loop fusion | bytes 114688
  26.8 1.4 %bitcast_dynamic-update-slice_fusion.2 = bf16[16,1,896,32]{2,3,1,0:T(8,128)(2,1)} fusion(bf16[16,1,896,32]{2,3,1,0:T(8,128)(2,1)} %bitcast_dynamic-update-slice_fusion.3, bf16[1,14336,32]{1,2,0:T(8,128)(2,1)} %param.11), kind=kLoop, calls=%fused_computation.7 | loop fusion | bytes 114688
  28.2 1.4 %bitcast_dynamic-update-slice_fusion.1 = bf16[16,1,896,32]{2,3,1,0:T(8,128)(2,1)} fusion(bf16[16,1,896,32]{2,3,1,0:T(8,128)(2,1)} %bitcast_dynamic-update-slice_fusion.2, bf16[1,14336,32]{1,2,0:T(8,128)(2,1)} %param.11), kind=kLoop, calls=%fused_computation.6 | loop fusion | bytes 114688
  29.6 1.5 %bitcast_dynamic-update-slice_fusion = bf16[16,1,896,32]{2,3,1,0:T(8,128)(2,1)} fusion(bf16[16,1,896,32]{2,3,1,0:T(8,128)(2,1)} %bitcast_dynamic-update-slice_fusion.1, bf16[1,14336,32]{1,2,0:T(8,128)(2,1)} %param.11), kind=kLoop, calls=%fused_computation.5 | loop fusion | bytes 114688 | tf_op jit(solution)/shard_map/stack | solution.py:11
  31.1 6.5 %all-to-all-start = ((bf16[16,1,896,32]{2,3,1,0:T(8,128)(2,1)}), bf16[16,1,896,32]{2,3,1,0:T(8,128)(2,1)S(1)}, u32[]{:S(2)}, u32[]{:S(2)}) async-start(bf16[16,1,896,32]{2,3,1,0:T(8,128)(2,1)} %bitcast_dynamic-update-slice_fusion), calls=%async_computation | async-start | bytes 1835008 | tf_op jit(solution)/shard_map/all_to_all | solution.py:10
  37.6 22.3 %all-gather.6.cloned.1.call-done = bf16[16,12,4096]{2,1,0:T(8,128)(2,1)} async-done(((bf16[1,12,4096]{2,1,0:T(8,128)(2,1)}), bf16[16,12,4096]{2,1,0:T(8,128)(2,1)}) %all-gather.6.cloned.1.call-update) | async-done | bytes 1572880 | tf_op jit(solution)/shard_map/all_gather | solution.py:8
  59.9 2.5 %reshape.11 = bf16[192,4096]{1,0:T(8,128)(2,1)S(1)} reshape(bf16[16,12,4096]{2,1,0:T(8,128)(2,1)} %all-gather.6.cloned.1.call-done) | data formatting | bytes 3145728
  62.3 4.9 %fusion.4 = f32[192,896]{1,0:T(8,128)S(1)} fusion(bf16[192,4096]{1,0:T(8,128)(2,1)S(1)} %reshape.11, bf16[4096,896]{1,0:T(8,128)(2,1)} %param.8), kind=kOutput, calls=%fused_computation.22 | convolution fusion | flops 1409286144 | bytes 9601024 | tf_op jit(solution)/shard_map/dot_general | solution.py:19
  67.3 5.0 %convolution_multiply_fusion = f32[192,896]{1,0:T(8,128)S(1)} fusion(bf16[192,4096]{1,0:T(8,128)(2,1)S(1)} %reshape.11, bf16[4096,896]{1,0:T(8,128)(2,1)} %param.9, f32[192,896]{1,0:T(8,128)S(1)} %fusion.4), kind=kOutput, calls=%fused_computation | convolution fusion | flops 1410146304 | bytes 10289152 | tf_op jit(solution)/shard_map/dot_general | solution.py:20
  72.3 1.1 fusion.5
  73.4 31.0 %fusion = f32[16,512]{1,0:T(8,128)S(1)} fusion(f32[192,512]{1,0:T(8,128)S(1)} %fusion.5), kind=kCustom, calls=%all-reduce-scatter | all-reduce-scatter fusion | flops 131073 | bytes 426496
  104.4 2.8 %collective-permute-start = (f32[16,512]{1,0:T(8,128)S(1)}, f32[16,512]{1,0:T(8,128)S(1)}, u32[]{:S(2)}, u32[]{:S(2)}) collective-permute-start(f32[16,512]{1,0:T(8,128)S(1)} %fusion), channel_id=1, source_target_pairs={{0,1},{1,2},{2,3},{3,4},{4,5},{5,6},{6,7},{7,8},{8,9},{9,10},{10,1... | collective-permute-start | bytes 98312
  107.2 2.9 %collective-permute-start.1 = (f32[16,512]{1,0:T(8,128)S(1)}, f32[16,512]{1,0:T(8,128)S(1)}, u32[]{:S(2)}, u32[]{:S(2)}) collective-permute-start(f32[16,512]{1,0:T(8,128)S(1)} %fusion), channel_id=1, source_target_pairs={{0,2},{1,3},{2,4},{3,5},{4,6},{5,7},{6,8},{7,9},{8,10},{9,11},{10,... | collective-permute-start | bytes 98312
  110.1 7.5 %collective-permute-start.2 = (f32[16,512]{1,0:T(8,128)S(1)}, f32[16,512]{1,0:T(8,128)S(1)}, u32[]{:S(2)}, u32[]{:S(2)}) collective-permute-start(f32[16,512]{1,0:T(8,128)S(1)} %fusion), channel_id=1, source_target_pairs={{0,3},{1,4},{2,5},{3,6},{4,7},{5,8},{6,9},{7,10},{8,11},{9,12},{10... | collective-permute-start | bytes 98312
  117.6 1.9 %collective-permute-start.3 = (f32[12,512]{1,0:T(8,128)S(1)}, f32[12,512]{1,0:T(8,128)S(1)}, u32[]{:S(2)}, u32[]{:S(2)}) collective-permute-start(f32[12,512]{1,0:T(8,128)S(1)} %slice), channel_id=1, source_target_pairs={{0,4},{1,5},{2,6},{3,7},{4,8},{5,9},{6,10},{7,11},{8,12},{9,13},{1... | collective-permute-start | bytes 73736
  120.8 1.5 %collective-permute-done.3 = f32[12,512]{1,0:T(8,128)S(1)} collective-permute-done((f32[12,512]{1,0:T(8,128)S(1)}, f32[12,512]{1,0:T(8,128)S(1)}, u32[]{:S(2)}, u32[]{:S(2)}) %collective-permute-start.3) | collective-permute-done | bytes 24608
  123.0 5.1 %fusion.3 = f32[12,16]{0,1:T(8,128)S(1)} fusion(f32[12,16,32]{2,1,0:T(8,128)S(1)} %reshape.9, bf16[16,4096,32]{1,2,0:T(8,128)(2,1)} %all-gather.4.cloned.1.call-done, bf16[12,4096]{1,0:T(8,128)(2,1)S(1)} %copy-done), kind=kOutput, calls=%fused_computation.4 | convolution fusion | flops 50343744 | bytes 4317952 | tf_op jit(solution)/shard_map/td,kdr->tkr/dot_general | solution.py:30
  128.0 0.7 copy.9
  (16 shorter events, 1.3 us)
Async XLA Ops:
  6.5 116.4 %copy-start = (bf16[12,4096]{1,0:T(8,128)(2,1)S(1)}, bf16[12,4096]{1,0:T(8,128)(2,1)}, u32[]{:S(2)}) copy-start(bf16[12,4096]{1,0:T(8,128)(2,1)} %param.7) | copy-start | bytes 294916
  6.5 53.4 %all-gather.6.cloned.1.call-start = ((), (), s32[]{:S(2)}) async-start(), calls=%async_computation.2 | async-start | bytes 2228224 | tf_op jit(solution)/shard_map/all_gather | solution.py:8
  7.3 115.7 %all-gather.4.cloned.1.call-start = ((), (), s32[]{:S(2)}) async-start(), calls=%async_computation.1 | async-start | bytes 4456448 | tf_op jit(solution)/shard_map/all_gather | solution.py:33
  31.1 41.2 %all-to-all-start = ((bf16[16,1,896,32]{2,3,1,0:T(8,128)(2,1)}), bf16[16,1,896,32]{2,3,1,0:T(8,128)(2,1)S(1)}, u32[]{:S(2)}, u32[]{:S(2)}) async-start(bf16[16,1,896,32]{2,3,1,0:T(8,128)(2,1)} %bitcast_dynamic-update-slice_fusion), calls=%async_computation | async-start | bytes 1835008 | tf_op jit(solution)/shard_map/all_to_all | solution.py:10
  67.3 52.3 %copy-start.1 = (u32[32]{0:T(128)S(1)}, u32[32]{0:T(128)}, u32[]{:S(2)}) copy-start(u32[32]{0:T(128)} %constant.11) | copy-start | bytes 388
  104.4 17.9 %collective-permute-start = (f32[16,512]{1,0:T(8,128)S(1)}, f32[16,512]{1,0:T(8,128)S(1)}, u32[]{:S(2)}, u32[]{:S(2)}) collective-permute-start(f32[16,512]{1,0:T(8,128)S(1)} %fusion), channel_id=1, source_target_pairs={{0,1},{1,2},{2,3},{3,4},{4,5},{5,6},{6,7},{7,8},{8,9},{9,10},{10,1... | collective-permute-start | bytes 98312
  107.2 15.1 %collective-permute-start.1 = (f32[16,512]{1,0:T(8,128)S(1)}, f32[16,512]{1,0:T(8,128)S(1)}, u32[]{:S(2)}, u32[]{:S(2)}) collective-permute-start(f32[16,512]{1,0:T(8,128)S(1)} %fusion), channel_id=1, source_target_pairs={{0,2},{1,3},{2,4},{3,5},{4,6},{5,7},{6,8},{7,9},{8,10},{9,11},{10,... | collective-permute-start | bytes 98312
  110.1 12.2 %collective-permute-start.2 = (f32[16,512]{1,0:T(8,128)S(1)}, f32[16,512]{1,0:T(8,128)S(1)}, u32[]{:S(2)}, u32[]{:S(2)}) collective-permute-start(f32[16,512]{1,0:T(8,128)S(1)} %fusion), channel_id=1, source_target_pairs={{0,3},{1,4},{2,5},{3,6},{4,7},{5,8},{6,9},{7,10},{8,11},{9,12},{10... | collective-permute-start | bytes 98312
  117.6 4.7 %collective-permute-start.3 = (f32[12,512]{1,0:T(8,128)S(1)}, f32[12,512]{1,0:T(8,128)S(1)}, u32[]{:S(2)}, u32[]{:S(2)}) collective-permute-start(f32[12,512]{1,0:T(8,128)S(1)} %slice), channel_id=1, source_target_pairs={{0,4},{1,5},{2,6},{3,7},{4,8},{5,9},{6,10},{7,11},{8,12},{9,13},{1... | collective-permute-start | bytes 73736
Sparse Core Ops, SparseCore 0:
  9.5 50.3 all-gather.5
  62.0 54.0 all-gather.3
